TPU v7x, 32 devices: a whole 2x2x4 slice. The times are simulated.
32 devices in a mesh: gx: 8 (over z, y), gy: 4 (over x, core).
Axes of the slice: x: 2, y: 2, z: 4, core: 2. Of those that a mesh axis runs over, the one named last changes fastest.
Arguments:
- tracer: float32 [128, 256, 512], P(None, 'gx', 'gy'), may hold values from -11 to 11
- velocity: float32 [2, 256, 512], P(None, 'gx', 'gy'), may hold values from -0.25 to 0.25
- diffusivity: float32 [128], replicated, may hold values from 0.02 to 0.08
- singular: float32 [94], replicated, may hold values from 0.5 to 8
- basis_vectors: float32 [94, 2, 256, 512], P(None, None, 'gx', 'gy'), may hold values from -10 to 10, as said below
Outputs:
- tracer_next: float32 [128, 256, 512], P(None, 'gx', 'gy')
- basis_next: float32 [96, 2, 256, 512], P(None, None, 'gx', 'gy')
Inputs may be any that keep to these rules, and one draw needn't show every extreme that they name: The 94 vectors basis_vectors[i], each over all 2 x 256 x 512 cells, are orthogonal with squared length 262144, to float32 rounding.
All inputs are finite; a program needn't handle non-finite values.
Results may differ from a plain program's by a relative error of at most 0.0003.
Values sent between devices are 32-bit elements; how exact they have to be, the bound alone decides.
A program may use at most 64 MiB of HBM per device.

v0:
```python
import functools
import math

import jax
import jax.numpy as jnp
from jax import lax
from jax.experimental import pallas as pl
from jax.experimental.pallas import tpu as pltpu
from jax.sharding import PartitionSpec as P

ROOT_ITERS = 5
MESH = pl.DeviceIdType.MESH
F32 = jnp.float32
HIGHEST = lax.Precision.HIGHEST
PAD = 8
GROUP = 8


def core_root_rows(sums, singular, count_all, width):
    n = width
    k = n - 2
    lane = lax.broadcasted_iota(jnp.int32, (1, 128), 1)
    in_basis = lane < k
    total = sums * (1.0 / count_all)
    first, second = total[0:1], total[1:2]

    def pick(row, where):
        return jnp.sum(jnp.where(lane == where, row, 0.0), axis=1, keepdims=True)

    p1 = jnp.where(in_basis, first, 0.0)
    p2 = jnp.where(in_basis, second, 0.0)
    g11 = pick(first, k) - jnp.sum(p1 * p1, axis=1, keepdims=True) + 1e-6
    g12 = pick(first, k + 1) - jnp.sum(p1 * p2, axis=1, keepdims=True)
    g22 = pick(second, k + 1) - jnp.sum(p2 * p2, axis=1, keepdims=True) + 1e-6
    r11 = jnp.sqrt(g11)
    r12 = g12 / r11
    r22 = jnp.sqrt(g22 - r12 * r12)
    e1 = jnp.where(lane == k, 1.0, 0.0)
    e2 = jnp.where(lane == k + 1, 1.0, 0.0)
    v1 = p1 + r11 * e1
    v2 = p2 + r12 * e1 + r22 * e2
    squares = singular * singular
    scale = jnp.sum(squares + v1 * v1 + v2 * v2, axis=1, keepdims=True) / n
    inv_scale = 1.0 / scale
    diagonal = squares * inv_scale
    u1 = v1 * jnp.sqrt(inv_scale)
    u2 = v2 * jnp.sqrt(inv_scale)

    count = 2**ROOT_ITERS
    half = count // 2
    row = lax.broadcasted_iota(jnp.int32, (half, 1), 0)
    shifts = jnp.ones((half, 1), F32)
    for j in range(1, half):
        shifts = jnp.where(row == j - 1, math.tan(math.pi * j / count) ** 2, shifts)
    real = row < half - 1
    inverse = 1.0 / (diagonal + shifts)
    a1 = inverse * u1
    a2 = inverse * u2
    m11 = 1.0 + jnp.sum(a1 * u1, axis=1, keepdims=True)
    m12 = jnp.sum(a1 * u2, axis=1, keepdims=True)
    m22 = 1.0 + jnp.sum(a2 * u2, axis=1, keepdims=True)
    weight = 2.0 * (1.0 + shifts) / count
    ratio = m12 / m11
    top = jnp.sqrt(weight * shifts / m11)
    low = jnp.sqrt(weight * shifts / (m22 - m12 * ratio))
    z1 = jnp.where(real, a1 * top, u1 * (1.0 / math.sqrt(count)))
    z2 = jnp.where(real, (a2 - ratio * a1) * low, u2 * (1.0 / math.sqrt(count)))
    straight = (1.0 + diagonal) / count + jnp.sum(
        jnp.where(real, weight * inverse, 0.0), axis=0, keepdims=True
    ) * diagonal
    wide = jnp.concatenate([z1, z2, jnp.zeros((128 - count, 128), F32)], axis=0)
    tall = wide.T
    root = jnp.dot(tall, wide, precision=HIGHEST, preferred_element_type=F32)
    square_row = lax.broadcasted_iota(jnp.int32, (128, 128), 0)
    square_lane = lax.broadcasted_iota(jnp.int32, (128, 128), 1)
    root = (root + jnp.where(square_row == square_lane, straight, 0.0)) * jnp.sqrt(scale)
    w1 = (e1 - p1) / r11
    w2 = (e2 - p2 - r12 * w1) / r22
    mixed = jnp.where(square_lane < k, root, 0.0) + root[:, k : k + 1] * w1 + root[:, k + 1 : k + 2] * w2
    return mixed[:n, :n]


def kernel(
    nx, ny, diffusivity, velocity, singular, tracer, basis,
    out_tracer, out_basis,
    pad0, pad1, wpad, done, bas, outb, coef, acc,
    xs0, xr0, ys0, yr0, xsw, xrw, ysw, yrw, xs1, xr1, ys1, yr1,
    part, from_x, mid, from_y, spad, cmat,
    in_sem, halo_s, halo_r, gx_s, gx_r, gy_s, gy_r, out_sem, fin_sem,
):
    levels, height, lanes = tracer.shape
    k, window = basis.shape[0], basis.shape[1]
    n = k + 2
    rows = window * height
    gx, gy = lax.axis_index("gx"), lax.axis_index("gy")
    count_all = float(rows * lanes * nx * ny)

    load_tracer = pltpu.make_async_copy(tracer, pad0.at[:, PAD : PAD + height, :], in_sem.at[0])
    load_basis = pltpu.make_async_copy(basis, bas.at[:k], in_sem.at[1])
    load_tracer.start()
    load_basis.start()

    barrier = pltpu.get_barrier_semaphore()

    def greet_x(i, c):
        pl.semaphore_signal(barrier, inc=1, device_id=(lax.rem(gx + i, nx), gy), device_id_type=MESH)
        return c

    def greet_y(i, c):
        pl.semaphore_signal(barrier, inc=1, device_id=(gx, lax.rem(gy + i, ny)), device_id_type=MESH)
        return c

    lax.fori_loop(1, nx, greet_x, 0)
    lax.fori_loop(1, ny, greet_y, 0)

    vx, vy = velocity[0], velocity[1]
    coef[0] = 1.0 - jnp.abs(vx) - jnp.abs(vy)
    coef[1] = jnp.maximum(vx, 0.0)
    coef[2] = jnp.maximum(-vx, 0.0)
    coef[3] = jnp.maximum(vy, 0.0)
    coef[4] = jnp.maximum(-vy, 0.0)
    spad[...] = jnp.zeros_like(spad)
    spad[0:1, 0:k] = singular[...]
    acc[...] = jnp.zeros_like(acc)

    lane = lax.broadcasted_iota(jnp.int32, (height, lanes), 1)
    right_x, left_x = lax.rem(gx + 1, nx), lax.rem(gx + nx - 1, nx)
    right_y, left_y = lax.rem(gy + 1, ny), lax.rem(gy + ny - 1, ny)

    def halos(xs, xr, ys, yr, base):
        out = []
        for slot, (src, dst, device) in enumerate(
            [
                (xs.at[0], xr.at[0], (right_x, gy)),
                (xs.at[1], xr.at[1], (left_x, gy)),
                (ys.at[0], yr.at[0], (gx, right_y)),
                (ys.at[1], yr.at[1], (gx, left_y)),
            ]
        ):
            out.append(
                pltpu.make_async_remote_copy(
                    src_ref=src, dst_ref=dst, send_sem=halo_s.at[base + slot], recv_sem=halo_r.at[base + slot],
                    device_id=device, device_id_type=MESH,
                )
            )
        return out

    def pack(z, tile, high, low):
        here = lane == z
        return (
            jnp.where(here, pltpu.roll(tile, lax.rem(z + 1, lanes), 1), high),
            jnp.where(here, pltpu.roll(tile, z, 1), low),
        )

    def advance(centre, west, east, below, above, south_edge, north_edge, d):
        south = jnp.where(lane == 0, south_edge, pltpu.roll(centre, 1, 1))
        north = jnp.where(lane == lanes - 1, north_edge, pltpu.roll(centre, lanes - 1, 1))
        spread = (west + east) + (south + north) + (below + above)
        return (
            centre * (coef[0] - 6.0 * d)
            + (west * coef[1] + east * coef[2])
            + (south * coef[3] + north * coef[4])
            + d * spread
        )

    def edges(yr, z):
        return (
            pltpu.roll(yr[0], lax.rem(lanes - z, lanes), 1),
            pltpu.roll(yr[1], lanes - 1 - z, 1),
        )

    mid_rows = pl.ds(PAD, height)
    west_rows = pl.ds(PAD - 1, height)
    east_rows = pl.ds(PAD + 1, height)

    def level_of(src, yr, z):
        zb, za = lax.rem(z + levels - 1, levels), lax.rem(z + 1, levels)
        south_edge, north_edge = edges(yr, z)
        return advance(
            src[z, mid_rows, :], src[z, west_rows, :], src[z, east_rows, :],
            src[zb, mid_rows, :], src[za, mid_rows, :],
            south_edge, north_edge, diffusivity[z],
        )

    full = PAD + height + PAD
    flat0 = pad0.reshape(levels * full, lanes)
    flat1 = pad1.reshape(levels * full, lanes)
    zero = jnp.zeros((height, lanes), F32)

    load_tracer.wait()
    high, low = lax.fori_loop(
        0, levels, lambda z, c: pack(z, pad0[z, mid_rows, :], *c), (zero, zero), unroll=4
    )
    ys0[0], ys0[1] = high, low
    xs0[0] = flat0[pl.ds(PAD + height - 1, levels, stride=full), :]
    xs0[1] = flat0[pl.ds(PAD, levels, stride=full), :]
    pl.semaphore_wait(barrier, nx + ny - 2)
    first = halos(xs0, xr0, ys0, yr0, 0)
    for copy in first:
        copy.start()
    for copy in first:
        copy.wait_recv()
    flat0[pl.ds(PAD - 1, levels, stride=full), :] = xr0[0]
    flat0[pl.ds(PAD + height, levels, stride=full), :] = xr0[1]

    high, low = zero, zero
    for j in range(window + 2):
        z = (j - 1) % levels
        tile = level_of(pad0, yr0, z)
        wpad[j, mid_rows, :] = tile
        xsw[0, j : j + 1, :] = tile[height - 1 : height]
        xsw[1, j : j + 1, :] = tile[0:1]
        high, low = pack(j, tile, high, low)
    ysw[0], ysw[1] = high, low
    second = halos(xsw, xrw, ysw, yrw, 4)
    for copy in second:
        copy.start()

    def one(z, c):
        tile = level_of(pad0, yr0, z)
        pad1[z, mid_rows, :] = tile
        return pack(z, tile, *c)

    high, low = lax.fori_loop(0, levels, one, (zero, zero), unroll=2)
    ys1[0], ys1[1] = high, low
    xs1[0] = flat1[pl.ds(PAD + height - 1, levels, stride=full), :]
    xs1[1] = flat1[pl.ds(PAD, levels, stride=full), :]
    third = halos(xs1, xr1, ys1, yr1, 8)
    for copy in third:
        copy.start()

    for copy in second:
        copy.wait_recv()
    for j in range(1, window + 1):
        wpad[j, PAD - 1 : PAD, :] = xrw[0, j : j + 1, :]
        wpad[j, PAD + height : PAD + height + 1, :] = xrw[1, j : j + 1, :]
    load_basis.wait()
    for j in range(1, window + 1):
        south_edge, north_edge = edges(yrw, j)
        tile = advance(
            wpad[j, mid_rows, :], wpad[j, west_rows, :], wpad[j, east_rows, :],
            wpad[j - 1, mid_rows, :], wpad[j + 1, mid_rows, :],
            south_edge, north_edge, diffusivity[j - 1],
        )
        bas[k, j - 1] = wpad[j, mid_rows, :]
        bas[k + 1, j - 1] = tile

    def products(i, c):
        for m in range(2):
            total = jnp.zeros((8, lanes), F32)
            for w in range(window):
                value = bas[i, w] * bas[k + m, w]
                for r in range(height // 8):
                    total = total + value[8 * r : 8 * r + 8]
            acc[m, pl.ds(i, 1), :] = jnp.sum(total, axis=0, keepdims=True)
        return c

    lax.fori_loop(0, n, products, 0, unroll=4)
    ones = jnp.ones((8, lanes), F32)
    for m in range(2):
        row = lax.dot_general(
            ones, acc[m], (((1,), (1,)), ((), ())), precision=HIGHEST, preferred_element_type=F32
        )
        part[4 * m : 4 * m + 4, :] = row[0:4]

    def copy_x(i):
        peer = lax.rem(gx + i, nx)
        return pltpu.make_async_remote_copy(
            src_ref=part, dst_ref=from_x.at[gx], send_sem=gx_s.at[peer], recv_sem=gx_r.at[gx],
            device_id=(peer, gy), device_id_type=MESH,
        )

    def arrived_x(i):
        peer = lax.rem(gx + i, nx)
        return pltpu.make_async_remote_copy(
            src_ref=part, dst_ref=from_x.at[peer], send_sem=gx_s.at[peer], recv_sem=gx_r.at[peer],
            device_id=(peer, gy), device_id_type=MESH,
        )

    def copy_y(i):
        peer = lax.rem(gy + i, ny)
        return pltpu.make_async_remote_copy(
            src_ref=mid, dst_ref=from_y.at[gy], send_sem=gy_s.at[peer], recv_sem=gy_r.at[gy],
            device_id=(gx, peer), device_id_type=MESH,
        )

    def arrived_y(i):
        peer = lax.rem(gy + i, ny)
        return pltpu.make_async_remote_copy(
            src_ref=mid, dst_ref=from_y.at[peer], send_sem=gy_s.at[peer], recv_sem=gy_r.at[peer],
            device_id=(gx, peer), device_id_type=MESH,
        )

    def do(count, act):
        def body(i, c):
            act(i)
            return c

        lax.fori_loop(1, count, body, 0)

    from_x[gx] = part[...]
    do(nx, lambda i: copy_x(i).start())

    for copy in third:
        copy.wait_recv()
    flat1[pl.ds(PAD - 1, levels, stride=full), :] = xr1[0]
    flat1[pl.ds(PAD + height, levels, stride=full), :] = xr1[1]

    def two(z, c):
        done[z] = level_of(pad1, yr1, z)
        return c

    half = levels // 2
    lax.fori_loop(0, half, two, 0, unroll=2)
    store0 = pltpu.make_async_copy(done.at[:half], out_tracer.at[:half], out_sem.at[0])
    store0.start()

    do(nx, lambda i: arrived_x(i).wait_recv())
    total = from_x[0]
    for i in range(1, nx):
        total = total + from_x[i]
    mid[...] = total
    from_y[gy] = total
    do(ny, lambda i: copy_y(i).start())

    lax.fori_loop(half, levels, two, 0, unroll=2)
    store1 = pltpu.make_async_copy(done.at[half:], out_tracer.at[half:], out_sem.at[1])
    store1.start()

    do(ny, lambda i: arrived_y(i).wait_recv())
    total = from_y[0]
    for i in range(1, ny):
        total = total + from_y[i]
    sums = jnp.concatenate([total[0:1], total[4:5]], axis=0)
    cmat[...] = core_root_rows(sums, spad[0:1], count_all, n)

    flat_bas = bas.reshape(n * rows, lanes)
    flat_out = outb.reshape(n * rows, lanes)
    per = height // GROUP
    stores = []
    for g in range(rows // GROUP):
        def rotate(q, c):
            r = g * GROUP + 2 * q
            cols = jnp.concatenate(
                [flat_bas[pl.ds(r, n, stride=rows), :], flat_bas[pl.ds(r + 1, n, stride=rows), :]], axis=1
            )
            out = jnp.dot(cmat[...], cols, precision=HIGHEST, preferred_element_type=F32)
            flat_out[pl.ds(r, n, stride=rows), :] = out[:, :lanes]
            flat_out[pl.ds(r + 1, n, stride=rows), :] = out[:, lanes:]
            return c

        lax.fori_loop(0, GROUP // 2, rotate, 0, unroll=True)
        span = pl.ds((g % per) * GROUP, GROUP)
        store = pltpu.make_async_copy(
            outb.at[:, g // per, span, :], out_basis.at[:, g // per, span, :], fin_sem.at[g]
        )
        store.start()
        stores.append(store)

    for copy in first + second + third:
        copy.wait_send()
    do(nx, lambda i: copy_x(i).wait_send())
    do(ny, lambda i: copy_y(i).wait_send())
    store0.wait()
    store1.wait()
    for store in stores:
        store.wait()


def on_device(nx, ny, tracer, velocity, diffusivity, singular, basis_vectors):
    levels, height, lanes = tracer.shape
    k, window = basis_vectors.shape[0], basis_vectors.shape[1]
    n = k + 2
    full = PAD + height + PAD
    vmem = lambda *shape: pltpu.VMEM(shape, F32)
    dma = lambda *shape: pltpu.SemaphoreType.DMA(shape)
    any_space = pl.BlockSpec(memory_space=pl.ANY)
    return pl.pallas_call(
        functools.partial(kernel, nx, ny),
        out_shape=(
            jax.ShapeDtypeStruct((levels, height, lanes), F32),
            jax.ShapeDtypeStruct((n, window, height, lanes), F32),
        ),
        in_specs=[
            pl.BlockSpec(memory_space=pltpu.SMEM),
            pl.BlockSpec(memory_space=pltpu.VMEM),
            pl.BlockSpec(memory_space=pltpu.VMEM),
            any_space,
            any_space,
        ],
        out_specs=(any_space, any_space),
        scratch_shapes=[
            vmem(levels, full, lanes), vmem(levels, full, lanes), vmem(window + 2, full, lanes),
            vmem(levels, height, lanes), vmem(n, window, height, lanes), vmem(n, window, height, lanes),
            vmem(5, height, lanes), vmem(2, 128, lanes),
            vmem(2, levels, lanes), vmem(2, levels, lanes), vmem(2, height, lanes), vmem(2, height, lanes),
            vmem(2, 8, lanes), vmem(2, 8, lanes), vmem(2, height, lanes), vmem(2, height, lanes),
            vmem(2, levels, lanes), vmem(2, levels, lanes), vmem(2, height, lanes), vmem(2, height, lanes),
            vmem(8, lanes), vmem(nx, 8, lanes), vmem(8, lanes), vmem(ny, 8, lanes), vmem(8, 128), vmem(n, n),
            dma(2), dma(12), dma(12), dma(nx), dma(nx), dma(ny), dma(ny), dma(2), dma(window * height // GROUP),
        ],
        compiler_params=pltpu.CompilerParams(
            collective_id=0, has_side_effects=True, vmem_limit_bytes=48 * 1024 * 1024
        ),
    )(diffusivity, velocity, singular.reshape(1, k), tracer, basis_vectors)


def solution(mesh):
    return jax.shard_map(
        functools.partial(on_device, mesh.shape["gx"], mesh.shape["gy"]),
        mesh=mesh,
        in_specs=(P(None, "gx", "gy"), P(None, "gx", "gy"), P(), P(), P(None, None, "gx", "gy")),
        out_specs=(P(None, "gx", "gy"), P(None, None, "gx", "gy")),
        check_vma=False,
    )
```

profile of v0, /device:TPU:0, one launch (start us, length us, event | category | flops | bytes accessed | tf_op | source)
XLA Modules:
  0.0 52.0 jit_solution(13168007065853818604)
XLA Ops:
  0.6 0.0 copy-start
  0.6 1.6 %copy-done = f32[128,32,128]{2,1,0:T(8,128)S(1)} copy-done((f32[128,32,128]{2,1,0:T(8,128)S(1)}, f32[128,32,128]{2,1,0:T(8,128)}, u32[]{:S(2)}) %copy-start) | copy-done | bytes 2097176
  2.2 0.0 copy-start.1
  2.2 0.8 %copy-done.1 = f32[2,32,128]{2,1,0:T(8,128)S(1)} copy-done((f32[2,32,128]{2,1,0:T(8,128)S(1)}, f32[2,32,128]{2,1,0:T(8,128)}, u32[]{:S(2)}) %copy-start.1) | copy-done | bytes 32792
  3.0 0.0 copy-start.2
  3.0 0.7 %copy-done.2 = f32[128]{0:T(128)S(1)} copy-done((f32[128]{0:T(128)S(1)}, f32[128]{0:T(128)}, u32[]{:S(2)}) %copy-start.2) | copy-done | bytes 536
  3.6 0.0 copy-start.3
  3.6 0.7 %copy-done.3 = f32[94]{0:T(128)S(1)} copy-done((f32[94]{0:T(128)S(1)}, f32[94]{0:T(128)}, u32[]{:S(2)}) %copy-start.3) | copy-done | bytes 400
  4.3 43.4 %shard_map.68 = (f32[128,32,128]{2,1,0:T(8,128)S(1)}, f32[96,2,32,128]{3,2,1,0:T(8,128)}) custom-call(f32[128]{0:T(128)S(1)} %copy-done.2, f32[2,32,128]{2,1,0:T(8,128)S(1)} %copy-done.1, f32[1,94]{1,0:T(1,128)S(1)} %bitcast.1, f32[128,32,128]{2,1,0:T(8,128)S(1)} %copy-done, f32[94,2,32,128]{3,2,1,0:T(8,128)} %basis.1), custom_call_target="tpu_custom_call" | custom-call | tf_op jit(solution)/shard_map/pallas_call | solution.py:378
  47.7 0.0 copy-start.4
  47.7 1.3 %copy.9 = f32[128,32,128]{2,1,0:T(8,128)} copy(f32[128,32,128]{2,1,0:T(8,128)S(1)} %get-tuple-element.4) | data formatting | bytes 4194304
  49.1 1.3 %copy-done.4 = f32[96,2,32,128]{3,2,1,0:T(8,128)S(1)} copy-done((f32[96,2,32,128]{3,2,1,0:T(8,128)S(1)}, f32[96,2,32,128]{3,2,1,0:T(8,128)}, u32[]{:S(2)}) %copy-start.4) | copy-done | bytes 3145752
  50.4 1.7 %copy.10 = f32[96,2,32,128]{3,2,1,0:T(8,128)} copy(f32[96,2,32,128]{3,2,1,0:T(8,128)S(1)} %copy-done.4) | data formatting | bytes 6291456
Async XLA Ops:
  0.6 1.6 %copy-start = (f32[128,32,128]{2,1,0:T(8,128)S(1)}, f32[128,32,128]{2,1,0:T(8,128)}, u32[]{:S(2)}) copy-start(f32[128,32,128]{2,1,0:T(8,128)} %tracer.1) | copy-start | bytes 6291460
  2.2 0.8 %copy-start.1 = (f32[2,32,128]{2,1,0:T(8,128)S(1)}, f32[2,32,128]{2,1,0:T(8,128)}, u32[]{:S(2)}) copy-start(f32[2,32,128]{2,1,0:T(8,128)} %velocity.1) | copy-start | bytes 98308
  3.0 0.7 %copy-start.2 = (f32[128]{0:T(128)S(1)}, f32[128]{0:T(128)}, u32[]{:S(2)}) copy-start(f32[128]{0:T(128)} %diffusivity.1) | copy-start | bytes 1540
  3.6 0.7 %copy-start.3 = (f32[94]{0:T(128)S(1)}, f32[94]{0:T(128)}, u32[]{:S(2)}) copy-start(f32[94]{0:T(128)} %param.8) | copy-start | bytes 1132
  47.7 2.6 %copy-start.4 = (f32[96,2,32,128]{3,2,1,0:T(8,128)S(1)}, f32[96,2,32,128]{3,2,1,0:T(8,128)}, u32[]{:S(2)}) copy-start(f32[96,2,32,128]{3,2,1,0:T(8,128)} %get-tuple-element.5) | copy-start | bytes 9437188
where the time goes:
time: 52.3 us; the launch traced here: 52 us
  Pallas kernels  43.4 us (83%)
  local copies, waits for them, and re-layouts  7.95 us (15%)
  between operations  0.66 us (1%)
    pallas_call x1, Pallas kernels, on_device(): pl.pallas_call(functools.partial(kernel, nx, ny), out_shape=(jax.ShapeDty...  43.4 us
    unnamed x12, local copies, waits for them, and re-layouts  7.95 us

commit v1 on v0

--- a/solution.py
+++ b/solution.py
@@ -81,9 +81,9 @@
 
 
 def kernel(
-    nx, ny, diffusivity, velocity, singular, tracer, basis,
+    nx, ny, diffusivity, drow, velocity, singular, tracer, basis,
     out_tracer, out_basis,
-    pad0, pad1, wpad, done, bas, outb, coef, acc,
+    pad0, pad1, dtile, done, bas, outb, coef, acc,
     xs0, xr0, ys0, yr0, xsw, xrw, ysw, yrw, xs1, xr1, ys1, yr1,
     part, from_x, mid, from_y, spad, cmat,
     in_sem, halo_s, halo_r, gx_s, gx_r, gy_s, gy_r, out_sem, fin_sem,
@@ -145,17 +145,44 @@
             )
         return out
 
-    def pack(z, tile, high, low):
-        here = lane == z
-        return (
-            jnp.where(here, pltpu.roll(tile, lax.rem(z + 1, lanes), 1), high),
-            jnp.where(here, pltpu.roll(tile, z, 1), low),
-        )
-
-    def advance(centre, west, east, below, above, south_edge, north_edge, d):
-        south = jnp.where(lane == 0, south_edge, pltpu.roll(centre, 1, 1))
-        north = jnp.where(lane == lanes - 1, north_edge, pltpu.roll(centre, lanes - 1, 1))
-        spread = (west + east) + (south + north) + (below + above)
+    own_edge = (lane == 0) | (lane == lanes - 1)
+    odd_lane = lax.rem(lane, 2) == 1
+    sub = lax.broadcasted_iota(jnp.int32, (height, lanes), 0)
+    mid_rows = pl.ds(PAD, height)
+    west_rows = pl.ds(PAD - 1, height)
+    east_rows = pl.ds(PAD + 1, height)
+    full = PAD + height + PAD
+    flat0 = pad0.reshape(levels * full, lanes)
+    flat1 = pad1.reshape(levels * full, lanes)
+    flat2 = done.reshape(levels * height, lanes)
+    zero = jnp.zeros((height, lanes), F32)
+    edge_zero = jnp.zeros((levels, lanes), F32)
+    for flat in (flat0, flat1):
+        flat[pl.ds(PAD - 1, levels, stride=full), :] = edge_zero
+        flat[pl.ds(PAD + height, levels, stride=full), :] = edge_zero
+    dtile[...] = jnp.broadcast_to(drow[...], (lanes, lanes)).T
+
+    def pack(z, tile, into):
+        here = (lane == z) | (lane == lax.rem(z + lanes - 1, lanes))
+        return jnp.where(here, pltpu.roll(tile, z, 1), into)
+
+    def apart(even, odd):
+        low = jnp.where(odd_lane, odd, even)
+        high = pltpu.roll(jnp.where(odd_lane, even, odd), 1, 1)
+        return high, low
+
+    def together(low, high):
+        high = pltpu.roll(high, lanes - 1, 1)
+        return jnp.where(odd_lane, high, low), jnp.where(odd_lane, low, high)
+
+    def inner(src, z):
+        d = diffusivity[z]
+        zb, za = lax.rem(z + levels - 1, levels), lax.rem(z + 1, levels)
+        centre = src[z, mid_rows, :]
+        west, east = src[z, west_rows, :], src[z, east_rows, :]
+        south = jnp.where(lane == 0, 0.0, pltpu.roll(centre, 1, 1))
+        north = jnp.where(lane == lanes - 1, 0.0, pltpu.roll(centre, lanes - 1, 1))
+        spread = (west + east) + (south + north) + (src[zb, mid_rows, :] + src[za, mid_rows, :])
         return (
             centre * (coef[0] - 6.0 * d)
             + (west * coef[1] + east * coef[2])
@@ -163,87 +190,100 @@
             + d * spread
         )
 
-    def edges(yr, z):
+    def add_rows(flat, begin, step, xr):
+        low_row = pl.ds(begin, levels, stride=step)
+        high_row = pl.ds(begin + height - 1, levels, stride=step)
+        flat[low_row, :] = flat[low_row, :] + xr[0] * (coef[1, 0:1, :] + dtile[...])
+        flat[high_row, :] = flat[high_row, :] + xr[1] * (coef[2, height - 1 : height, :] + dtile[...])
+
+    def column_terms(yr):
+        low = yr[0] * (coef[3][:, 0:1] + drow[...])
+        high = yr[1] * (coef[4][:, lanes - 1 : lanes] + drow[...])
+        return together(low, high)
+
+    def add_columns(tile, z, terms):
+        return tile + jnp.where(own_edge, pltpu.roll(terms, lax.rem(lanes - z, lanes), 1), 0.0)
+
+    load_tracer.wait()
+
+    def pack_pair(q, c):
         return (
-            pltpu.roll(yr[0], lax.rem(lanes - z, lanes), 1),
-            pltpu.roll(yr[1], lanes - 1 - z, 1),
-        )
-
-    mid_rows = pl.ds(PAD, height)
-    west_rows = pl.ds(PAD - 1, height)
-    east_rows = pl.ds(PAD + 1, height)
-
-    def level_of(src, yr, z):
-        zb, za = lax.rem(z + levels - 1, levels), lax.rem(z + 1, levels)
-        south_edge, north_edge = edges(yr, z)
-        return advance(
-            src[z, mid_rows, :], src[z, west_rows, :], src[z, east_rows, :],
-            src[zb, mid_rows, :], src[za, mid_rows, :],
-            south_edge, north_edge, diffusivity[z],
-        )
-
-    full = PAD + height + PAD
-    flat0 = pad0.reshape(levels * full, lanes)
-    flat1 = pad1.reshape(levels * full, lanes)
-    zero = jnp.zeros((height, lanes), F32)
-
-    load_tracer.wait()
-    high, low = lax.fori_loop(
-        0, levels, lambda z, c: pack(z, pad0[z, mid_rows, :], *c), (zero, zero), unroll=4
-    )
-    ys0[0], ys0[1] = high, low
+            pack(2 * q, pad0[2 * q, mid_rows, :], c[0]),
+            pack(2 * q + 1, pad0[2 * q + 1, mid_rows, :], c[1]),
+        )
+
     xs0[0] = flat0[pl.ds(PAD + height - 1, levels, stride=full), :]
     xs0[1] = flat0[pl.ds(PAD, levels, stride=full), :]
     pl.semaphore_wait(barrier, nx + ny - 2)
     first = halos(xs0, xr0, ys0, yr0, 0)
-    for copy in first:
+    for copy in first[:2]:
         copy.start()
+    ys0[0], ys0[1] = apart(*lax.fori_loop(0, levels // 2, pack_pair, (zero, zero), unroll=4))
+    for copy in first[2:]:
+        copy.start()
+
+    def one(z, c):
+        pad1[z, mid_rows, :] = inner(pad0, z)
+        return c
+
+    lax.fori_loop(0, levels, one, 0, unroll=8)
+
     for copy in first:
         copy.wait_recv()
-    flat0[pl.ds(PAD - 1, levels, stride=full), :] = xr0[0]
-    flat0[pl.ds(PAD + height, levels, stride=full), :] = xr0[1]
-
-    high, low = zero, zero
-    for j in range(window + 2):
-        z = (j - 1) % levels
-        tile = level_of(pad0, yr0, z)
-        wpad[j, mid_rows, :] = tile
-        xsw[0, j : j + 1, :] = tile[height - 1 : height]
-        xsw[1, j : j + 1, :] = tile[0:1]
-        high, low = pack(j, tile, high, low)
-    ysw[0], ysw[1] = high, low
+    add_rows(flat1, PAD, full, xr0)
+    terms = column_terms(yr0)
+
+    def finish(z, parity, c):
+        tile = add_columns(pad1[z, mid_rows, :], z, terms[parity])
+        pad1[z, mid_rows, :] = tile
+        c = list(c)
+        c[parity] = pack(z, tile, c[parity])
+        return tuple(c)
+
+    packed = (zero, zero)
+    for z in [levels - 1] + list(range(window + 1)):
+        packed = finish(z, z % 2, packed)
+    ysw[0], ysw[1] = apart(*packed)
+    xsw[0] = flat1[pl.ds(PAD + height - 1, 8, stride=full), :]
+    xsw[1] = flat1[pl.ds(PAD, 8, stride=full), :]
     second = halos(xsw, xrw, ysw, yrw, 4)
     for copy in second:
         copy.start()
 
-    def one(z, c):
-        tile = level_of(pad0, yr0, z)
-        pad1[z, mid_rows, :] = tile
-        return pack(z, tile, *c)
-
-    high, low = lax.fori_loop(0, levels, one, (zero, zero), unroll=2)
-    ys1[0], ys1[1] = high, low
+    begin = window + 1
+
+    def finish_pair(q, c):
+        z = begin + 2 * q
+        return finish(z + 1, (begin + 1) % 2, finish(z, begin % 2, c))
+
+    packed = lax.fori_loop(0, (levels - 1 - begin) // 2, finish_pair, packed, unroll=2)
+    ys1[0], ys1[1] = apart(*packed)
     xs1[0] = flat1[pl.ds(PAD + height - 1, levels, stride=full), :]
     xs1[1] = flat1[pl.ds(PAD, levels, stride=full), :]
     third = halos(xs1, xr1, ys1, yr1, 8)
     for copy in third:
         copy.start()
 
+    def two(z, c):
+        done[z] = inner(pad1, z)
+        return c
+
+    quarter, half = levels // 4, levels // 2
+    lax.fori_loop(0, quarter, two, 0, unroll=8)
+
+    load_basis.wait()
     for copy in second:
         copy.wait_recv()
-    for j in range(1, window + 1):
-        wpad[j, PAD - 1 : PAD, :] = xrw[0, j : j + 1, :]
-        wpad[j, PAD + height : PAD + height + 1, :] = xrw[1, j : j + 1, :]
-    load_basis.wait()
-    for j in range(1, window + 1):
-        south_edge, north_edge = edges(yrw, j)
-        tile = advance(
-            wpad[j, mid_rows, :], wpad[j, west_rows, :], wpad[j, east_rows, :],
-            wpad[j - 1, mid_rows, :], wpad[j + 1, mid_rows, :],
-            south_edge, north_edge, diffusivity[j - 1],
-        )
-        bas[k, j - 1] = wpad[j, mid_rows, :]
-        bas[k + 1, j - 1] = tile
+    window_terms = column_terms(yrw)
+    for z in range(window):
+        d = diffusivity[z]
+        tile = add_columns(done[z], z, window_terms[z % 2])
+        tile = tile + jnp.where(sub == 0, xrw[0, z : z + 1, :] * (coef[1, 0:1, :] + d), 0.0)
+        tile = tile + jnp.where(
+            sub == height - 1, xrw[1, z : z + 1, :] * (coef[2, height - 1 : height, :] + d), 0.0
+        )
+        bas[k, z] = pad1[z, mid_rows, :]
+        bas[k + 1, z] = tile
 
     def products(i, c):
         for m in range(2):
@@ -301,19 +341,7 @@
     from_x[gx] = part[...]
     do(nx, lambda i: copy_x(i).start())
 
-    for copy in third:
-        copy.wait_recv()
-    flat1[pl.ds(PAD - 1, levels, stride=full), :] = xr1[0]
-    flat1[pl.ds(PAD + height, levels, stride=full), :] = xr1[1]
-
-    def two(z, c):
-        done[z] = level_of(pad1, yr1, z)
-        return c
-
-    half = levels // 2
-    lax.fori_loop(0, half, two, 0, unroll=2)
-    store0 = pltpu.make_async_copy(done.at[:half], out_tracer.at[:half], out_sem.at[0])
-    store0.start()
+    lax.fori_loop(quarter, half + quarter, two, 0, unroll=8)
 
     do(nx, lambda i: arrived_x(i).wait_recv())
     total = from_x[0]
@@ -323,7 +351,22 @@
     from_y[gy] = total
     do(ny, lambda i: copy_y(i).start())
 
-    lax.fori_loop(half, levels, two, 0, unroll=2)
+    lax.fori_loop(half + quarter, levels, two, 0, unroll=8)
+    for copy in third:
+        copy.wait_recv()
+    add_rows(flat2, 0, height, xr1)
+    last_terms = column_terms(yr1)
+
+    def close_pair(q, c):
+        for parity in range(2):
+            z = 2 * q + parity
+            done[z] = add_columns(done[z], z, last_terms[parity])
+        return c
+
+    lax.fori_loop(0, half // 2, close_pair, 0, unroll=4)
+    store0 = pltpu.make_async_copy(done.at[:half], out_tracer.at[:half], out_sem.at[0])
+    store0.start()
+    lax.fori_loop(half // 2, half, close_pair, 0, unroll=4)
     store1 = pltpu.make_async_copy(done.at[half:], out_tracer.at[half:], out_sem.at[1])
     store1.start()
 
@@ -385,12 +428,13 @@
             pl.BlockSpec(memory_space=pltpu.SMEM),
             pl.BlockSpec(memory_space=pltpu.VMEM),
             pl.BlockSpec(memory_space=pltpu.VMEM),
+            pl.BlockSpec(memory_space=pltpu.VMEM),
             any_space,
             any_space,
         ],
         out_specs=(any_space, any_space),
         scratch_shapes=[
-            vmem(levels, full, lanes), vmem(levels, full, lanes), vmem(window + 2, full, lanes),
+            vmem(levels, full, lanes), vmem(levels, full, lanes), vmem(lanes, lanes),
             vmem(levels, height, lanes), vmem(n, window, height, lanes), vmem(n, window, height, lanes),
             vmem(5, height, lanes), vmem(2, 128, lanes),
             vmem(2, levels, lanes), vmem(2, levels, lanes), vmem(2, height, lanes), vmem(2, height, lanes),
@@ -400,9 +444,9 @@
             dma(2), dma(12), dma(12), dma(nx), dma(nx), dma(ny), dma(ny), dma(2), dma(window * height // GROUP),
         ],
         compiler_params=pltpu.CompilerParams(
-            collective_id=0, has_side_effects=True, vmem_limit_bytes=48 * 1024 * 1024
+            collective_id=0, has_side_effects=True, vmem_limit_bytes=60 * 1024 * 1024
         ),
-    )(diffusivity, velocity, singular.reshape(1, k), tracer, basis_vectors)
+    )(diffusivity, diffusivity.reshape(1, levels), velocity, singular.reshape(1, k), tracer, basis_vectors)
 
 
 def solution(mesh):

time: 52.3 us -> 38.8 us (0.74)
  Pallas kernels: 43.4 us -> 33.1 us
  local copies, waits for them, and re-layouts: 7.95 us -> 4.91 us
    pallas_call x1, Pallas kernels: 43.4 us -> 33.1 us  [on_device(): pl.pallas_call(functools.partial(kernel, nx, ny), out_shape=(jax.ShapeDty...]
    unnamed x12 -> x4, local copies, waits for them, and re-layouts: 7.95 us -> 4.91 us
where the time goes in v1:
time: 38.8 us; the launch traced here: 38.6 us
  Pallas kernels  33.1 us (85%)
  local copies, waits for them, and re-layouts  4.91 us (13%)
  between operations  0.65 us (2%)
    pallas_call x1, Pallas kernels, on_device(): pl.pallas_call(functools.partial(kernel, nx, ny), out_shape=(jax.ShapeDty...  33.1 us
    unnamed x4, local copies, waits for them, and re-layouts  4.91 us

profile of v1, /device:TPU:0, one launch (start us, length us, event | category | flops | bytes accessed | tf_op | source)
XLA Modules:
  0.0 38.6 jit_solution(11727831247075582994)
XLA Ops:
  0.6 33.1 %shard_map.68 = (f32[128,32,128]{2,1,0:T(8,128)}, f32[96,2,32,128]{3,2,1,0:T(8,128)}) custom-call(f32[128]{0:T(128)} %diffusivity.1, f32[1,128]{1,0:T(1,128)} %bitcast.2, f32[2,32,128]{2,1,0:T(8,128)} %velocity.1, f32[1,94]{1,0:T(1,128)} %bitcast.3, f32[128,32,128]{2,1,0:T(8,128)} %tracer.1, f32[94,2,32,128]{3,2,1,0:T(8,128)} %basis.1), custom_call_target="tpu_custom_call" | custom-call | tf_op jit(solution)/shard_map/pallas_call | solution.py:421
  33.7 0.0 copy-start
  33.7 3.2 %copy.9 = f32[128,32,128]{2,1,0:T(8,128)} copy(f32[128,32,128]{2,1,0:T(8,128)} %get-tuple-element.4) | data formatting | bytes 4194304
  37.0 0.0 copy-done
  37.0 1.7 %copy.10 = f32[96,2,32,128]{3,2,1,0:T(8,128)} copy(f32[96,2,32,128]{3,2,1,0:T(8,128)S(1)} %copy-done) | data formatting | bytes 6291456
Async XLA Ops:
  33.7 3.3 %copy-start = (f32[96,2,32,128]{3,2,1,0:T(8,128)S(1)}, f32[96,2,32,128]{3,2,1,0:T(8,128)}, u32[]{:S(2)}) copy-start(f32[96,2,32,128]{3,2,1,0:T(8,128)} %get-tuple-element.5) | copy-start | bytes 9437188

commit v2 on v1

--- a/solution.py
+++ b/solution.py
@@ -11,6 +11,7 @@
 ROOT_ITERS = 5
 MESH = pl.DeviceIdType.MESH
 F32 = jnp.float32
+BF16 = jnp.bfloat16
 HIGHEST = lax.Precision.HIGHEST
 PAD = 8
 GROUP = 8
@@ -82,11 +83,11 @@
 
 def kernel(
     nx, ny, diffusivity, drow, velocity, singular, tracer, basis,
-    out_tracer, out_basis,
-    pad0, pad1, dtile, done, bas, outb, coef, acc,
+    done, bas, cmat,
+    pad0, pad1, dtile, coef, acc,
     xs0, xr0, ys0, yr0, xsw, xrw, ysw, yrw, xs1, xr1, ys1, yr1,
-    part, from_x, mid, from_y, spad, cmat,
-    in_sem, halo_s, halo_r, gx_s, gx_r, gy_s, gy_r, out_sem, fin_sem,
+    part, from_x, mid, from_y, spad,
+    in_sem, halo_s, halo_r, gx_s, gx_r, gy_s, gy_r,
 ):
     levels, height, lanes = tracer.shape
     k, window = basis.shape[0], basis.shape[1]
@@ -364,11 +365,7 @@
         return c
 
     lax.fori_loop(0, half // 2, close_pair, 0, unroll=4)
-    store0 = pltpu.make_async_copy(done.at[:half], out_tracer.at[:half], out_sem.at[0])
-    store0.start()
     lax.fori_loop(half // 2, half, close_pair, 0, unroll=4)
-    store1 = pltpu.make_async_copy(done.at[half:], out_tracer.at[half:], out_sem.at[1])
-    store1.start()
 
     do(ny, lambda i: arrived_y(i).wait_recv())
     total = from_y[0]
@@ -377,9 +374,22 @@
     sums = jnp.concatenate([total[0:1], total[4:5]], axis=0)
     cmat[...] = core_root_rows(sums, spad[0:1], count_all, n)
 
+    for copy in first + second + third:
+        copy.wait_send()
+    do(nx, lambda i: copy_x(i).wait_send())
+    do(ny, lambda i: copy_y(i).wait_send())
+
+
+def finish_kernel(done, bas, cmat, out_tracer, out_basis, outb, out_sem, fin_sem):
+    n, window, height, lanes = bas.shape
+    rows = window * height
+    store0 = pltpu.make_async_copy(done, out_tracer, out_sem)
+    store0.start()
     flat_bas = bas.reshape(n * rows, lanes)
     flat_out = outb.reshape(n * rows, lanes)
     per = height // GROUP
+    coarse = cmat[...].astype(BF16)
+    stacked = jnp.concatenate([coarse, (cmat[...] - coarse.astype(F32)).astype(BF16)], axis=0)
     stores = []
     for g in range(rows // GROUP):
         def rotate(q, c):
@@ -387,7 +397,10 @@
             cols = jnp.concatenate(
                 [flat_bas[pl.ds(r, n, stride=rows), :], flat_bas[pl.ds(r + 1, n, stride=rows), :]], axis=1
             )
-            out = jnp.dot(cmat[...], cols, precision=HIGHEST, preferred_element_type=F32)
+            high = cols.astype(BF16)
+            rest = (cols - high.astype(F32)).astype(BF16)
+            both = jnp.dot(stacked, high, preferred_element_type=F32)
+            out = (jnp.dot(stacked[:n], rest, preferred_element_type=F32) + both[n:]) + both[:n]
             flat_out[pl.ds(r, n, stride=rows), :] = out[:, :lanes]
             flat_out[pl.ds(r + 1, n, stride=rows), :] = out[:, lanes:]
             return c
@@ -400,12 +413,7 @@
         store.start()
         stores.append(store)
 
-    for copy in first + second + third:
-        copy.wait_send()
-    do(nx, lambda i: copy_x(i).wait_send())
-    do(ny, lambda i: copy_y(i).wait_send())
     store0.wait()
-    store1.wait()
     for store in stores:
         store.wait()
 
@@ -418,35 +426,38 @@
     vmem = lambda *shape: pltpu.VMEM(shape, F32)
     dma = lambda *shape: pltpu.SemaphoreType.DMA(shape)
     any_space = pl.BlockSpec(memory_space=pl.ANY)
+    vmem_space = pl.BlockSpec(memory_space=pltpu.VMEM)
+    done, bas, cmat = pl.pallas_call(
+        functools.partial(kernel, nx, ny),
+        out_shape=(vmem(levels, height, lanes), vmem(n, window, height, lanes), vmem(n, n)),
+        in_specs=[pl.BlockSpec(memory_space=pltpu.SMEM), vmem_space, vmem_space, vmem_space, any_space, any_space],
+        out_specs=(vmem_space, vmem_space, vmem_space),
+        scratch_shapes=[
+            vmem(levels, full, lanes), vmem(levels, full, lanes), vmem(lanes, lanes),
+            vmem(5, height, lanes), vmem(2, 128, lanes),
+            vmem(2, levels, lanes), vmem(2, levels, lanes), vmem(2, height, lanes), vmem(2, height, lanes),
+            vmem(2, 8, lanes), vmem(2, 8, lanes), vmem(2, height, lanes), vmem(2, height, lanes),
+            vmem(2, levels, lanes), vmem(2, levels, lanes), vmem(2, height, lanes), vmem(2, height, lanes),
+            vmem(8, lanes), vmem(nx, 8, lanes), vmem(8, lanes), vmem(ny, 8, lanes), vmem(8, 128),
+            dma(2), dma(12), dma(12), dma(nx), dma(nx), dma(ny), dma(ny),
+        ],
+        compiler_params=pltpu.CompilerParams(
+            collective_id=0, has_side_effects=True, vmem_limit_bytes=56 * 1024 * 1024
+        ),
+    )(diffusivity, diffusivity.reshape(1, levels), velocity, singular.reshape(1, k), tracer, basis_vectors)
     return pl.pallas_call(
-        functools.partial(kernel, nx, ny),
+        finish_kernel,
         out_shape=(
             jax.ShapeDtypeStruct((levels, height, lanes), F32),
             jax.ShapeDtypeStruct((n, window, height, lanes), F32),
         ),
-        in_specs=[
-            pl.BlockSpec(memory_space=pltpu.SMEM),
-            pl.BlockSpec(memory_space=pltpu.VMEM),
-            pl.BlockSpec(memory_space=pltpu.VMEM),
-            pl.BlockSpec(memory_space=pltpu.VMEM),
-            any_space,
-            any_space,
-        ],
+        in_specs=[vmem_space, vmem_space, vmem_space],
         out_specs=(any_space, any_space),
         scratch_shapes=[
-            vmem(levels, full, lanes), vmem(levels, full, lanes), vmem(lanes, lanes),
-            vmem(levels, height, lanes), vmem(n, window, height, lanes), vmem(n, window, height, lanes),
-            vmem(5, height, lanes), vmem(2, 128, lanes),
-            vmem(2, levels, lanes), vmem(2, levels, lanes), vmem(2, height, lanes), vmem(2, height, lanes),
-            vmem(2, 8, lanes), vmem(2, 8, lanes), vmem(2, height, lanes), vmem(2, height, lanes),
-            vmem(2, levels, lanes), vmem(2, levels, lanes), vmem(2, height, lanes), vmem(2, height, lanes),
-            vmem(8, lanes), vmem(nx, 8, lanes), vmem(8, lanes), vmem(ny, 8, lanes), vmem(8, 128), vmem(n, n),
-            dma(2), dma(12), dma(12), dma(nx), dma(nx), dma(ny), dma(ny), dma(2), dma(window * height // GROUP),
+            vmem(n, window, height, lanes), pltpu.SemaphoreType.DMA, dma(window * height // GROUP),
         ],
-        compiler_params=pltpu.CompilerParams(
-            collective_id=0, has_side_effects=True, vmem_limit_bytes=60 * 1024 * 1024
-        ),
-    )(diffusivity, diffusivity.reshape(1, levels), velocity, singular.reshape(1, k), tracer, basis_vectors)
+        compiler_params=pltpu.CompilerParams(vmem_limit_bytes=16 * 1024 * 1024),
+    )(done, bas, cmat)
 
 
 def solution(mesh):

time: 38.8 us -> 32.6 us (0.84)
  local copies, waits for them, and re-layouts: 4.91 us -> 0 us
  Pallas kernels: 33.1 us -> 31.8 us
    unnamed x4 -> x0, local copies, waits for them, and re-layouts: 4.91 us -> none
    pallas_call x1 -> x2, Pallas kernels: 33.1 us -> 31.8 us  [the longest x1 27.1 us: on_device(): pl.pallas_call(functools.partial(kernel, nx, ny), out_shape=(vmem(levels,...]
where the time goes in v2:
time: 32.6 us; the launch traced here: 32.5 us
  Pallas kernels  31.8 us (98%)
  between operations  0.64 us (2%)
    pallas_call x1, Pallas kernels, on_device(): pl.pallas_call(functools.partial(kernel, nx, ny), out_shape=(vmem(levels,...  27.1 us
    pallas_call x1, Pallas kernels, on_device(): pl.pallas_call(finish_kernel, out_shape=(jax.ShapeDtypeStruct((levels, he...  4.71 us

profile of v2, /device:TPU:0, one launch (start us, length us, event | category | flops | bytes accessed | tf_op | source)
XLA Modules:
  0.0 32.5 jit_solution(1855054972675541546)
XLA Ops:
  0.6 27.1 %shard_map.68 = (f32[128,32,128]{2,1,0:T(8,128)S(1)}, f32[96,2,32,128]{3,2,1,0:T(8,128)S(1)}, f32[96,96]{1,0:T(8,128)S(1)}) custom-call(f32[128]{0:T(128)} %diffusivity.1, f32[1,128]{1,0:T(1,128)} %bitcast.2, f32[2,32,128]{2,1,0:T(8,128)} %velocity.1, f32[1,94]{1,0:T(1,128)} %bitcast.3, f32[128,32,128]{2,1,0:T(8,128)} %tracer.1, f32[94,2,32,128]{3,2,1,0:T(8,128)} %basis.1), custom_call_target="tpu_custom_call" | custom-call | tf_op jit(solution)/shard_map/pallas_call | solution.py:430
  27.7 4.7 %shard_map.69 = (f32[128,32,128]{2,1,0:T(8,128)}, f32[96,2,32,128]{3,2,1,0:T(8,128)}) custom-call(f32[128,32,128]{2,1,0:T(8,128)S(1)} %get-tuple-element.5.done, f32[96,2,32,128]{3,2,1,0:T(8,128)S(1)} %get-tuple-element.6.bas, f32[96,96]{1,0:T(8,128)S(1)} %get-tuple-element.7.cmat), custom_call_target="tpu_custom_call" | custom-call | tf_op jit(solution)/shard_map/pallas_call | solution.py:448
